TPU v7x, 32 devices: a whole 2x2x4 slice. The times are simulated.
32 devices in a mesh: band: 8 (over y, x, core), slab: 4 (over z).
Axes of the slice: x: 2, y: 2, z: 4, core: 2. Of those that a mesh axis runs over, the one named last changes fastest.
Arguments:
- orbitals: float32 [8, 128, 128, 128], P('band', 'slab'), may hold values from -6 to 6
- column_ids: int32 [4, 1536], P('slab'), may hold values from 0 to 4095, as said below
- source_ids: int32 [2], replicated, may hold values from 0 to 7
Outputs:
- exchange: float32 [8, 128, 128, 128], P('band', 'slab')
- energy: float32 [8, 6144], P('band', 'slab')
Inputs may be any that keep to these rules, and one draw needn't show every extreme that they name: `column_ids`: A column is numbered c = (ky + 32) * 64 + kz + 32. Every column with ky^2 + kz^2 < 32^2 appears exactly once in the whole table; every other slot holds 0, a column outside that disk. One row holds 1536 such disk columns.
All inputs are finite; a program needn't handle non-finite values.
Results may differ from a plain program's by a relative error of at most 0.0001.
Values sent between devices are 32-bit elements; how exact they have to be, the bound alone decides.
A program may use at most 128 MiB of HBM per device.

v0:
```python
import math

import jax
import jax.numpy as jnp
import numpy as np
from jax import lax
from jax.sharding import PartitionSpec as P

KCUT = 32
KB = 64


def from_root(shard, axis, root):
    mine = lax.axis_index(axis) == root
    return lax.psum(jnp.where(mine, shard, jnp.zeros_like(shard)), axis)


def fourier_tables(modes, points, offset):
    wave = jnp.arange(modes, dtype=jnp.int32) - offset
    point = jnp.arange(points, dtype=jnp.int32)
    phase = wave[:, None] * point[None, :] % points
    angle = phase.astype(jnp.float32) * (2.0 * math.pi / points)
    return (jnp.cos(angle), jnp.sin(angle))


def column_kernel(slot_ids):
    wave_y = slot_ids // KB - KCUT
    wave_z = slot_ids % KB - KCUT
    wave_x = jnp.arange(KB, dtype=jnp.int32) - KCUT
    radius = wave_x[:, None] ** 2 + (wave_y * wave_y + wave_z * wave_z)[None, :]
    return jnp.where(radius < KCUT * KCUT, 4.0 / (1.0 + radius.astype(jnp.float32) / 1024.0), 0.0)


def even_width(slabs):
    wave = np.arange(KB) - KCUT
    inside = int(np.sum(wave[:, None] ** 2 + wave[None, :] ** 2 < KCUT * KCUT))
    return -(-inside // (slabs * 128)) * 128


def pair_potentials(pair_block, send_ids, own_ids):
    precise = lax.Precision.HIGHEST
    pair_count, planes, points = (pair_block.shape[0], pair_block.shape[1], pair_block.shape[2])
    cos_table, sin_table = fourier_tables(KB, points, KCUT)
    unitary = float(points) ** (-1.5)
    forward_z = jnp.concatenate([cos_table.T, -sin_table.T], axis=1) * unitary
    along_z = jnp.dot(pair_block.reshape(-1, points), forward_z, precision=precise)
    along_z = along_z.reshape(pair_count, planes, points, 2 * KB)
    cos_part = jnp.einsum("ay,pxyb->pxab", cos_table, along_z, precision=precise)
    sin_part = jnp.einsum("ay,pxyb->pxab", sin_table, along_z, precision=precise)
    real_box = (cos_part[..., :KB] + sin_part[..., KB:]).reshape(pair_count, planes, KB * KB)
    imag_box = (cos_part[..., KB:] - sin_part[..., :KB]).reshape(pair_count, planes, KB * KB)
    real_cols = jnp.take(real_box, send_ids, axis=2)
    imag_cols = jnp.take(imag_box, send_ids, axis=2)
    col_width = own_ids.shape[0]
    kernel_table = column_kernel(own_ids)
    real_in = lax.all_to_all(real_cols, "slab", split_axis=2, concat_axis=1, tiled=True)
    imag_in = lax.all_to_all(imag_cols, "slab", split_axis=2, concat_axis=1, tiled=True)
    stacked = jnp.concatenate([real_in, imag_in], axis=2)
    cos_x = jnp.einsum("ax,pxw->paw", cos_table, stacked, precision=precise)
    sin_x = jnp.einsum("ax,pxw->paw", sin_table, stacked, precision=precise)
    real_k = cos_x[..., :col_width] + sin_x[..., col_width:]
    imag_k = cos_x[..., col_width:] - sin_x[..., :col_width]
    col_power = jnp.sum(kernel_table * (real_k * real_k + imag_k * imag_k), axis=1) / KB
    filtered = jnp.concatenate([kernel_table * real_k, kernel_table * imag_k], axis=2)
    cos_back = jnp.einsum("ax,paw->pxw", cos_table, filtered, precision=precise)
    sin_back = jnp.einsum("ax,paw->pxw", sin_table, filtered, precision=precise)
    real_x = cos_back[..., :col_width] - sin_back[..., col_width:]
    imag_x = cos_back[..., col_width:] + sin_back[..., :col_width]
    real_back, imag_back, col_power = (
        lax.all_to_all(real_x, "slab", split_axis=1, concat_axis=2, tiled=True),
        lax.all_to_all(imag_x, "slab", split_axis=1, concat_axis=2, tiled=True),
        col_power,
    )
    empty = jnp.zeros((pair_count, planes, KB * KB), jnp.float32)
    real_box = empty.at[:, :, send_ids].add(real_back).reshape(pair_count, planes, KB, KB)
    imag_box = empty.at[:, :, send_ids].add(imag_back).reshape(pair_count, planes, KB, KB)
    stacked = jnp.concatenate([real_box, imag_box], axis=3)
    cos_part = jnp.einsum("ay,pxab->pxyb", cos_table, stacked, precision=precise)
    sin_part = jnp.einsum("ay,pxab->pxyb", sin_table, stacked, precision=precise)
    real_y = cos_part[..., :KB] - sin_part[..., KB:]
    imag_y = cos_part[..., KB:] + sin_part[..., :KB]
    inverse_z = jnp.concatenate([cos_table, -sin_table], axis=0) * unitary
    joined = jnp.concatenate([real_y, imag_y], axis=3).reshape(-1, 2 * KB)
    potential = jnp.dot(joined, inverse_z, precision=precise).reshape(
        pair_count, planes, points, points
    )
    return (potential, col_power)


def body(orbitals, column_ids, source_ids):
    res_count = orbitals.shape[0]
    source_count = source_ids.shape[0]
    slabs = lax.axis_size("slab")
    capacity = column_ids.shape[1]
    listed = lax.all_gather(column_ids, "slab", axis=0, tiled=True).reshape(-1)
    per_owner = even_width(slabs)
    slot_total = slabs * per_owner
    ranking = jnp.argsort((listed == 0).astype(jnp.int32), stable=True)
    packed = listed[ranking]
    if slot_total > packed.shape[0]:
        packed = jnp.concatenate([packed, jnp.zeros((slot_total - packed.shape[0],), jnp.int32)])
    send_ids = packed[:slot_total]
    own_ids = lax.dynamic_slice_in_dim(send_ids, lax.axis_index("slab") * per_owner, per_owner)
    exchange = jnp.zeros(orbitals.shape, jnp.float32)
    col_power = jnp.zeros((res_count, own_ids.shape[0]), jnp.float32)
    for step in range(source_count):
        wanted = source_ids[step]
        local_piece = lax.dynamic_index_in_dim(orbitals, wanted % res_count, 0, keepdims=False)
        source = from_root(local_piece, "band", wanted // res_count)
        potential, step_power = pair_potentials(source[None] * orbitals, send_ids, own_ids)
        exchange = exchange + source[None] * potential
        col_power = col_power + step_power
    full_power = lax.all_gather(col_power, "slab", axis=1, tiled=True)
    places = (
        jnp.zeros((listed.shape[0],), jnp.int32)
        .at[ranking]
        .set(jnp.arange(listed.shape[0], dtype=jnp.int32))
    )
    slots = lax.axis_index("slab") * capacity + jnp.arange(capacity, dtype=jnp.int32)
    located = places[slots]
    picked = jnp.take(full_power, jnp.minimum(located, slot_total - 1), axis=1)
    energy = jnp.where(located[None, :] < slot_total, picked, 0.0)
    return (exchange, energy)


def solution(mesh):
    placed = (P("band", "slab", None, None), P("slab", None), P())
    return jax.shard_map(
        body,
        mesh=mesh,
        in_specs=placed,
        out_specs=(P("band", "slab", None, None), P("band", "slab")),
        check_vma=False,
    )
```

profile of v0, /device:TPU:0, one launch (start us, length us, event | category | flops | bytes accessed | tf_op | source)
XLA Modules:
  0.0 534.9 jit_solution(7558961442265672830)
XLA Ops:
  9.8 4.2 select_bitcast_fusion.1
  14.7 14.8 %all-gather.1 = s32[4,1,1536]{2,1,0:T(1,128)S(1)} all-gather(s32[1,1,1536]{2,1,0:T(1,128)S(1)} %bitcast.282), channel_id=1, replica_groups=mesh['band'=8,'slab'=4] {'slab'}, dimensions={0}, use_global_device_ids=true | all-gather | bytes 30720 | tf_op jit(solution)/shard_map/all_gather | solution.py:95
  29.5 6.7 %sort.17 = (s32[6144]{0:T(1024)}, s32[6144]{0:T(1024)S(1)}) sort(s32[6144]{0:T(1024)S(1)} %compare_convert_fusion, s32[6144]{0:T(1024)S(1)} %iota.68), dimensions={0}, to_apply=%region_1.2 | sort | flops 79872 | bytes 98304 | tf_op jit(solution)/shard_map/jit(argsort)/sort | solution.py:98
  36.2 34.8 %gather_fusion = s32[6144]{0:T(1024)S(1)} fusion(s32[6144]{0:T(1024)S(1)} %bitcast.241, s32[6144]{0:T(1024)S(1)} %get-tuple-element.28), kind=kCustom, calls=%fused_computation.4 | custom fusion | bytes 73728 | tf_op jit(solution)/shard_map/gather | solution.py:99
  71.4 26.7 %all-reduce.3.cloned.1.call-done = (f32[32,128,128]{2,1,0:T(8,128)}, f32[32,128,128]{2,1,0:T(8,128)}) async-done(((f32[32,128,128]{2,1,0:T(8,128)}, f32[32,128,128]{2,1,0:T(8,128)}), (f32[32,128,128]{2,1,0:T(8,128)}, f32[32,128,128]{2,1,0:T(8,128)})) %all-reduce.3.cloned.1.call-update) | async-done | bytes 4194320 | tf_op jit(solution)/shard_map/psum | solution.py:15
  98.1 3.5 fusion.6
  104.8 2.0 fusion.8
  108.3 2.5 convolution_bitcast_fusion.15
  110.8 2.0 slice_add_fusion.1
  112.8 1.9 copy.131
  114.6 3.5 slice_add_fusion.3
  118.1 3.3 copy.127
  121.5 7.3 %gather_fusion.5 = f32[3584,32]{1,0:T(8,128)} fusion(f32[32,4096]{0,1:T(8,128)S(1)} %bitcast.242, s32[4096]{0:T(1024)S(1)} %pad_clamp_fusion), kind=kCustom, calls=%fused_computation.2.clone | custom fusion | bytes 931840 | tf_op jit(solution)/shard_map/jit(_take)/gather | solution.py:52
  128.8 9.0 %gather_fusion.4 = f32[3584,32]{1,0:T(8,128)} fusion(f32[32,4096]{0,1:T(8,128)} %bitcast.243, s32[4096]{0:T(1024)S(1)} %pad_clamp_fusion), kind=kCustom, calls=%fused_computation.1.clone | custom fusion | bytes 931840 | tf_op jit(solution)/shard_map/jit(_take)/gather | solution.py:53
  138.5 7.4 %gather_fusion.6 = f32[3584,32]{1,0:T(8,128)} fusion(f32[32,4096]{0,1:T(8,128)S(1)} %bitcast.245, s32[4096]{0:T(1024)S(1)} %pad_clamp_fusion), kind=kCustom, calls=%fused_computation.3.clone | custom fusion | bytes 931840 | tf_op jit(solution)/shard_map/jit(_take)/gather | solution.py:53
  146.6 7.3 %gather_fusion.3 = f32[3584,32]{1,0:T(8,128)} fusion(f32[32,4096]{0,1:T(8,128)S(1)} %bitcast.244, s32[4096]{0:T(1024)S(1)} %pad_clamp_fusion), kind=kCustom, calls=%fused_computation.clone | custom fusion | bytes 931840 | tf_op jit(solution)/shard_map/jit(_take)/gather | solution.py:52
  153.9 6.0 %bitcast_select_fusion.1 = (f32[1,32,3584]{1,2,0:T(8,128)}, f32[1,32,3584]{1,2,0:T(8,128)}, f32[1,32,3584]{1,2,0:T(8,128)}, f32[1,32,3584]{1,2,0:T(8,128)}) fusion(f32[3584,32]{1,0:T(8,128)} %gather_fusion.5, pred[3584]{0:T(1024)(128)(4,1)S(1)} %compare_and_fusion, f32[3584,32]{1,0:T(8,128)} %gather_fusion.4, f32[3584,32]{1,0:T(8,128)} %gather_fusion.6, ...), kind=kLoop, calls=%fused_computation.38 | loop fusion | flops 458752 | bytes 3673600 | tf_op jit(solution)/shard_map/jit(_take)/select_n | solution.py:52
  160.5 16.9 %reduce.7 = f32[3584,32]{1,0:T(8,128)S(1)} reduce(f32[3584,1,32]{2,1,0:T(1,128)} %bitcast.257, f32[]{:T(128)} %broadcast.574), dimensions={1}, to_apply=%bitcast.232.reduce_sub_computation | reduce | bytes 917508
  178.9 4.8 all-to-all-start.5
  183.7 16.9 %reduce.9 = f32[3584,32]{1,0:T(8,128)S(1)} reduce(f32[3584,1,32]{2,1,0:T(1,128)} %bitcast.256, f32[]{:T(128)} %broadcast.574), dimensions={1}, to_apply=%bitcast.234.reduce_sub_computation | reduce | bytes 917508
  202.2 5.1 all-to-all-start.4
  207.3 16.9 %reduce.11 = f32[3584,32]{1,0:T(8,128)S(1)} reduce(f32[3584,1,32]{2,1,0:T(1,128)} %bitcast.255, f32[]{:T(128)} %broadcast.574), dimensions={1}, to_apply=%bitcast.228.reduce_sub_computation | reduce | bytes 917508
  225.7 5.1 all-to-all-start.1
  230.8 16.9 %reduce.13 = f32[3584,32]{1,0:T(8,128)S(1)} reduce(f32[3584,1,32]{2,1,0:T(1,128)} %bitcast.254, f32[]{:T(128)} %broadcast.574), dimensions={1}, to_apply=%bitcast.230.reduce_sub_computation | reduce | bytes 917508
  249.3 5.5 %all-to-all-start = ((f32[4,1,28672]{2,1,0:T(1,128)}), f32[4,1,28672]{2,1,0:T(1,128)}, u32[]{:S(2)}, u32[]{:S(2)}) async-start(f32[4,1,28672]{2,1,0:T(1,128)} %reshape.520), calls=%async_computation | async-start | bytes 917504 | tf_op jit(solution)/shard_map/all_to_all | solution.py:56
  254.9 2.7 reduce.8
  257.6 3.8 reshape.523
  262.0 1.9 reduce.10
  264.0 2.8 reshape.525
  269.1 2.7 reduce.12
  271.8 3.8 reshape.519
  278.1 1.6 convolution_bitcast_fusion.4
  281.3 2.9 reduce.14
  284.2 2.8 reshape.521
  289.6 1.6 convolution_bitcast_fusion.2
  291.2 1.6 convolution_bitcast_fusion.3
  294.3 5.1 all-to-all-start.3
  300.6 9.5 %all-to-all-done.3 = f32[1,128,896]{2,0,1:T(1,128)S(1)} async-done(((f32[1,128,896]{2,0,1:T(1,128)}), f32[1,128,896]{2,0,1:T(1,128)S(1)}, u32[]{:S(2)}, u32[]{:S(2)}) %all-to-all-start.3) | async-done | bytes 458784 | tf_op jit(solution)/shard_map/all_to_all | solution.py:71
  310.1 3.9 all-to-all-start.2
  314.0 23.0 %scatter_custom_fusion.4 = s32[6144]{0:T(1024)S(1)} fusion(s32[6144]{0:T(1024)S(1)} %get-tuple-element.27, s32[6144]{0:T(1024)S(1)} %iota.70, s32[]{:T(128)} %constant.140.clone.1), kind=kCustom, calls=%fused_computation.139 | custom fusion | bytes 24580 | tf_op jit(solution)/shard_map/scatter | solution.py:117
  337.1 8.4 %gather_fusion.1 = s32[1536]{0:T(1024)S(1)} fusion(s32[6144]{0:T(1024)S(1)} %scatter_custom_fusion.4, s32[2048]{0:T(1024)S(1)} %pad_clamp_fusion.2), kind=kCustom, calls=%fused_computation.5 | custom fusion | bytes 18432 | tf_op jit(solution)/shard_map/gather | solution.py:120
  345.5 1.7 convolution_bitcast_fusion
  347.2 1.7 convolution_bitcast_fusion.1
  350.2 5.1 all-to-all-start.7
  356.8 8.9 %all-to-all-done.7 = f32[1,128,896]{2,0,1:T(1,128)S(1)} async-done(((f32[1,128,896]{2,0,1:T(1,128)}), f32[1,128,896]{2,0,1:T(1,128)S(1)}, u32[]{:S(2)}, u32[]{:S(2)}) %all-to-all-start.7) | async-done | bytes 458784 | tf_op jit(solution)/shard_map/all_to_all | solution.py:71
  365.7 4.1 all-to-all-start.6
  369.9 16.5 %all-gather.2 = f32[4,1,896]{2,1,0:T(1,128)S(1)} all-gather(f32[1,1,896]{2,1,0:T(1,128)S(1)} %reshape.479), channel_id=2, replica_groups=mesh['band'=8,'slab'=4] {'slab'}, dimensions={0}, use_global_device_ids=true | all-gather | bytes 17920 | tf_op jit(solution)/shard_map/all_gather | solution.py:113
  386.4 8.4 %gather_fusion.2 = f32[1536]{0:T(1024)S(1)} fusion(f32[3584]{0:T(1024)S(1)} %reshape.480, s32[2048]{0:T(1024)S(1)} %pad_clamp_fusion.1), kind=kCustom, calls=%fused_computation.6 | custom fusion | bytes 18432 | tf_op jit(solution)/shard_map/jit(_take)/gather | solution.py:121
  395.8 1.8 copy.103
  397.6 21.0 %scatter_custom_fusion.1 = f32[32,4096]{0,1:T(8,128)S(1)} fusion(s32[3584]{0:T(1024)S(1)} %get-tuple-element.30, f32[3584,32]{1,0:T(8,128)} %copy.103, f32[]{:T(128)} %constant.139.clone.1), kind=kCustom, calls=%fused_computation.63 | custom fusion | flops 114688 | bytes 524800 | tf_op jit(solution)/shard_map/scatter-add | solution.py:76
  421.5 21.6 %scatter_custom_fusion = f32[32,4096]{0,1:T(8,128)} fusion(s32[3584]{0:T(1024)S(1)} %get-tuple-element.30, f32[3584,32]{1,0:T(8,128)S(1)} %copy.99, f32[]{:T(128)} %constant.139.clone.1), kind=kCustom, calls=%fused_computation.65 | custom fusion | flops 114688 | bytes 524292 | tf_op jit(solution)/shard_map/scatter-add | solution.py:75
  443.2 2.6 copy.129
  446.2 1.8 copy.120
  448.0 22.1 %scatter_custom_fusion.3 = f32[32,4096]{0,1:T(8,128)} fusion(s32[3584]{0:T(1024)S(1)} %get-tuple-element.30, f32[3584,32]{1,0:T(8,128)} %copy.120, f32[]{:T(128)} %constant.139.clone.1), kind=kCustom, calls=%fused_computation.59 | custom fusion | flops 114688 | bytes 524800 | tf_op jit(solution)/shard_map/scatter-add | solution.py:76
  470.1 2.5 copy.136
  472.6 5.1 convolution_bitcast_fusion.10
  477.7 5.1 convolution_bitcast_fusion.11
  484.2 1.8 copy.116
  486.0 22.2 %scatter_custom_fusion.2 = f32[32,4096]{0,1:T(8,128)} fusion(s32[3584]{0:T(1024)S(1)} %get-tuple-element.30, f32[3584,32]{1,0:T(8,128)} %copy.116, f32[]{:T(128)} %constant.139.clone.1), kind=kCustom, calls=%fused_computation.61 | custom fusion | flops 114688 | bytes 524800 | tf_op jit(solution)/shard_map/scatter-add | solution.py:75
  508.2 2.5 copy.135
  510.7 3.8 convolution_bitcast_fusion.8
  514.5 3.8 convolution_bitcast_fusion.9
  519.2 3.7 fusion
  522.9 4.9 add_bitcast_fusion
  (108 shorter events, 36.8 us)
Async XLA Ops:
  7.2 91.0 %all-reduce.3.cloned.1.call-start = ((), (), s32[]{:S(2)}) async-start(), calls=%async_computation.8 | async-start | bytes 8388608 | tf_op jit(solution)/shard_map/psum | solution.py:15
  14.0 0.7 copy-start.15
  36.2 61.9 %copy-start = (f32[1,32,128,128]{3,2,1,0:T(8,128)S(1)}, f32[1,32,128,128]{3,2,1,0:T(8,128)}, u32[]{:S(2)}) copy-start(f32[1,32,128,128]{3,2,1,0:T(8,128)} %param.5) | copy-start | bytes 6291460
  103.2 1.6 copy-start.2
  128.8 9.0 %copy-start.6 = (f32[1,32,64,64]{3,2,1,0:T(8,128)S(1)}, f32[1,32,64,64]{3,2,1,0:T(8,128)}, u32[]{:S(2)}) copy-start(f32[1,32,64,64]{3,2,1,0:T(8,128)} %get-tuple-element.14) | copy-start | bytes 1572868
  138.5 7.4 %copy-start.7 = (f32[1,32,64,64]{3,2,1,0:T(8,128)S(1)}, f32[1,32,64,64]{3,2,1,0:T(8,128)}, u32[]{:S(2)}) copy-start(f32[1,32,64,64]{3,2,1,0:T(8,128)} %get-tuple-element.15) | copy-start | bytes 1572868
  178.9 23.3 %all-to-all-start.5 = ((f32[4,1,28672]{2,1,0:T(1,128)}), f32[4,1,28672]{2,1,0:T(1,128)S(1)}, u32[]{:S(2)}, u32[]{:S(2)}) async-start(f32[4,1,28672]{2,1,0:T(1,128)} %reshape.522), calls=%async_computation.5 | async-start | bytes 917504 | tf_op jit(solution)/shard_map/all_to_all | solution.py:57
  202.2 23.6 %all-to-all-start.4 = ((f32[4,1,28672]{2,1,0:T(1,128)}), f32[4,1,28672]{2,1,0:T(1,128)S(1)}, u32[]{:S(2)}, u32[]{:S(2)}) async-start(f32[4,1,28672]{2,1,0:T(1,128)} %reshape.524), calls=%async_computation.4 | async-start | bytes 917504 | tf_op jit(solution)/shard_map/all_to_all | solution.py:56
  225.7 23.5 %all-to-all-start.1 = ((f32[4,1,28672]{2,1,0:T(1,128)}), f32[4,1,28672]{2,1,0:T(1,128)S(1)}, u32[]{:S(2)}, u32[]{:S(2)}) async-start(f32[4,1,28672]{2,1,0:T(1,128)} %reshape.518), calls=%async_computation.1 | async-start | bytes 917504 | tf_op jit(solution)/shard_map/all_to_all | solution.py:57
  249.3 12.7 %copy-start.11 = (f32[4,1,28672]{2,1,0:T(1,128)}, f32[4,1,28672]{2,1,0:T(1,128)S(1)}, u32[]{:S(2)}) copy-start(f32[4,1,28672]{2,1,0:T(1,128)S(1)} %all-to-all-done.1) | copy-start | bytes 1376260
  249.3 32.1 %all-to-all-start = ((f32[4,1,28672]{2,1,0:T(1,128)}), f32[4,1,28672]{2,1,0:T(1,128)}, u32[]{:S(2)}, u32[]{:S(2)}) async-start(f32[4,1,28672]{2,1,0:T(1,128)} %reshape.520), calls=%async_computation | async-start | bytes 917504 | tf_op jit(solution)/shard_map/all_to_all | solution.py:56
  266.7 2.3 copy-start.12
  287.5 1.8 copy-start.13
  287.5 1.8 copy-start.14
  294.3 15.9 %all-to-all-start.3 = ((f32[1,128,896]{2,0,1:T(1,128)}), f32[1,128,896]{2,0,1:T(1,128)S(1)}, u32[]{:S(2)}, u32[]{:S(2)}) async-start(f32[1,128,896]{2,0,1:T(1,128)} %copy.101), calls=%async_computation.3 | async-start | bytes 917504 | tf_op jit(solution)/shard_map/all_to_all | solution.py:71
  310.1 40.1 %all-to-all-start.2 = ((f32[1,128,896]{2,0,1:T(1,128)}), f32[1,128,896]{2,0,1:T(1,128)S(1)}, u32[]{:S(2)}, u32[]{:S(2)}) async-start(f32[1,128,896]{2,0,1:T(1,128)} %copy.97), calls=%async_computation.2 | async-start | bytes 917504 | tf_op jit(solution)/shard_map/all_to_all | solution.py:70
  350.2 44.6 %copy-start.8 = (f32[1,128,896]{2,0,1:T(1,128)}, f32[1,128,896]{2,0,1:T(1,128)S(1)}, u32[]{:S(2)}) copy-start(f32[1,128,896]{2,0,1:T(1,128)S(1)} %all-to-all-done.2) | copy-start | bytes 1376260
  350.2 15.5 %all-to-all-start.7 = ((f32[1,128,896]{2,0,1:T(1,128)}), f32[1,128,896]{2,0,1:T(1,128)S(1)}, u32[]{:S(2)}, u32[]{:S(2)}) async-start(f32[1,128,896]{2,0,1:T(1,128)} %copy.118), calls=%async_computation.7 | async-start | bytes 917504 | tf_op jit(solution)/shard_map/all_to_all | solution.py:71
  365.7 20.6 %copy-start.9 = (f32[1,128,896]{2,0,1:T(1,128)}, f32[1,128,896]{2,0,1:T(1,128)S(1)}, u32[]{:S(2)}) copy-start(f32[1,128,896]{2,0,1:T(1,128)S(1)} %all-to-all-done.7) | copy-start | bytes 1376260
  365.7 117.0 %all-to-all-start.6 = ((f32[1,128,896]{2,0,1:T(1,128)}), f32[1,128,896]{2,0,1:T(1,128)}, u32[]{:S(2)}, u32[]{:S(2)}) async-start(f32[1,128,896]{2,0,1:T(1,128)} %copy.114), calls=%async_computation.6 | async-start | bytes 917504 | tf_op jit(solution)/shard_map/all_to_all | solution.py:70
  443.2 2.6 copy-start.10
  514.5 3.8 copy-start.4
  514.5 3.8 copy-start.5
  519.1 3.7 copy-start.1
  519.1 3.7 copy-start.3
Sparse Core Ops, SparseCore 0:
  14.2 83.9 all-reduce.2
where the time goes:
time: 540 us; the launch traced here: 535 us
  other arithmetic  190 us (35%)
  local copies, waits for them, and re-layouts  163 us (30%)
  matrix products  50.4 us (9%)
  waiting for transfers between devices  45.2 us (8%)
  starting transfers between devices  38.7 us (7%)
  blocking collectives  31.3 us (6%)
  between operations  16.3 us (3%)
    unnamed x4, other arithmetic  67.5 us
    scatter-add x2, other arithmetic, pair_potentials(): empty.at[:, :, send_ids].add(real_back).reshape(pair_count, planes, KB, KB)  43.8 us
    scatter-add x2, other arithmetic, pair_potentials(): empty.at[:, :, send_ids].add(imag_back).reshape(pair_count, planes, KB, KB)  43.1 us
    gather x1, local copies, waits for them, and re-layouts, body(): packed = listed[ranking]  34.8 us
    psum x1, waiting for transfers between devices, from_root(): return lax.psum(jnp.where(mine, shard, jnp.zeros_like(shard)), axis)  26.7 us
    unnamed x51, local copies, waits for them, and re-layouts  23 us
    scatter x1, local copies, waits for them, and re-layouts, body(): places = jnp.zeros((listed.shape[0],), jnp.int32).at[ranking].set(jnp.ara...  23 us
    all_to_all x2, waiting for transfers between devices, pair_potentials(): lax.all_to_all(imag_x, 'slab', split_axis=1, concat_axis=2, tiled=True)  18.4 us
  transfers between devices with their start and end apart: 9, of which 3 were waited for; matrix products, arithmetic and copies ran while one was open for 48% of the time, Pallas kernels for 0%

commit v1 on v0

v1 whole, which is shorter than its diff:
```python
import functools

import jax
import jax.numpy as jnp
import ml_dtypes
import numpy as np
from jax import lax
from jax.experimental import pallas as pl
from jax.experimental.pallas import tpu as pltpu
from jax.sharding import PartitionSpec as P

KCUT = 32
KB = 64
KH = 32
ROWS = 8
F32 = jnp.float32
BF16 = jnp.bfloat16


def halves(table):
    table = table.astype(np.float32)
    high = table.astype(ml_dtypes.bfloat16)
    low = (table - high.astype(np.float32)).astype(ml_dtypes.bfloat16)
    return high, low


def tables(points):
    wave = np.arange(KB) - KCUT
    angle = (wave[:, None] * np.arange(points)[None, :] % points) * (2.0 * np.pi / points)
    forward = np.concatenate([np.cos(angle), np.sin(angle)], axis=0)
    backward = np.concatenate([np.cos(angle).T, np.sin(angle).T], axis=1)
    angle = (np.arange(KH)[:, None] * np.arange(points)[None, :] % points) * (2.0 * np.pi / points)
    unitary = float(points) ** (-1.5)
    cos_z, sin_z = np.cos(angle) * unitary, np.sin(angle) * unitary
    none = np.zeros_like(cos_z)
    into = np.concatenate(
        [
            np.concatenate([cos_z, none, -sin_z, none], axis=0).T,
            np.concatenate([none, cos_z, none, -sin_z], axis=0).T,
        ],
        axis=0,
    )
    twice = np.where(np.arange(KH) == 0, 1.0, 2.0)[:, None]
    cos_b, sin_b = cos_z * twice, sin_z * twice
    out = np.concatenate(
        [
            np.concatenate([cos_b, none, -sin_b, none], axis=0),
            np.concatenate([none, cos_b, none, -sin_b], axis=0),
        ],
        axis=1,
    )
    fh, fl = halves(forward)
    bh, bl = halves(backward)
    ih, il = halves(into)
    oh, ol = halves(out)
    return (np.concatenate([fh, fl], 0), np.concatenate([bh, bl], 0), ih, il, oh, ol)


def split(value):
    high = value.astype(BF16)
    return high, (value - high.astype(F32)).astype(BF16)


def mm(a, b):
    return jnp.dot(a, b, preferred_element_type=F32)


def left_apply(table_ref, value):
    rows = table_ref.shape[0] // 2
    high, low = split(value)
    both = mm(table_ref[...], high)
    return both[:rows] + both[rows:] + mm(table_ref[:rows, :], low)


def swap_parts(value, sign):
    half = value.shape[1] // 2
    lane = lax.broadcasted_iota(jnp.int32, value.shape, 1)
    rolled = pltpu.roll(value, half, 1)
    return jnp.where(lane < half, sign * rolled, -sign * rolled)


def to_waves(table_ref, value):
    both = left_apply(table_ref, value)
    return both[:KB] + swap_parts(both[KB:], 1.0)


def to_points(table_ref, value):
    return left_apply(table_ref, jnp.concatenate([value, swap_parts(value, -1.0)], axis=0))


def kernel(
    slabs, orb, src, ids, fw, bw, zih, zil, zoh, zol, exch, energy,
    send1, recv1, send2, recv2, powers, s1, r1, s2, r2, sp, rp, own,
):
    planes, points = orb.shape[0], orb.shape[1]
    chunks = planes // ROWS
    width = KB // slabs
    me = lax.axis_index("slab")

    def peer(step):
        return {"slab": lax.rem(me + step, slabs)}

    barrier = pltpu.get_barrier_semaphore()
    for step in range(1, slabs):
        pl.semaphore_signal(barrier, inc=1, device_id=peer(step), device_id_type=pl.DeviceIdType.MESH)
    pl.semaphore_wait(barrier, slabs - 1)

    forward = []
    for chunk in range(chunks):

        def group(part, carry, chunk=chunk):
            base = chunk * ROWS + part * 4
            here = orb[pl.ds(base, 4)].reshape(4 * points, points)
            h0, l0 = split(src[0, pl.ds(base, 4)].reshape(4 * points, points) * here)
            h1, l1 = split(src[1, pl.ds(base, 4)].reshape(4 * points, points) * here)
            high = jnp.concatenate([h0, h1], axis=1)
            low = jnp.concatenate([l0, l1], axis=1)
            along_z = mm(high, zih[...]) + mm(low, zih[...]) + mm(high, zil[...])
            for q in range(4):
                waves = to_waves(fw, along_z[q * points : (q + 1) * points])
                send1[pl.ds(chunk * KB * ROWS + part * 4 + q, KB, stride=ROWS), :] = waves
            return carry

        lax.fori_loop(0, ROWS // 4, group, 0)
        for step in list(range(1, slabs)) + [0]:
            to = lax.rem(me + step, slabs)
            first = pl.multiple_of(chunk * KB * ROWS + to * (width * ROWS), 8)
            source = send1.at[pl.ds(first, width * ROWS)]
            target = recv1.at[me * chunks + chunk]
            if step == 0:
                copy = pltpu.make_async_copy(source, target, own.at[0, chunk])
            else:
                copy = pltpu.make_async_remote_copy(
                    source, target, s1.at[chunk, step], r1.at[chunk, step],
                    device_id=peer(step), device_id_type=pl.DeviceIdType.MESH,
                )
            copy.start()
            forward.append(copy)
    for copy in forward:
        copy.wait()

    lane_z = lax.broadcasted_iota(jnp.int32, (KB, 2 * KB), 1) & (KH - 1)
    wave_x = lax.broadcasted_iota(jnp.int32, (KB, 2 * KB), 0) - KCUT
    flat = wave_x * wave_x + lane_z * lane_z

    def column(k, carry):
        rows = pl.ds(pl.multiple_of(k * ROWS, ROWS), ROWS)
        spectrum = to_waves(fw, recv1[:, rows, :].reshape(points, 2 * KB))
        wave_y = me * width + k - KCUT
        radius = flat + wave_y * wave_y
        weight = jnp.where(radius < KCUT * KCUT, 4.0 / (1.0 + radius.astype(F32) / 1024.0), 0.0)
        filtered = weight * spectrum
        powers[me, pl.ds(k, 1), :] = jnp.sum(filtered * spectrum, axis=0, keepdims=True)
        send2[:, rows, :] = to_points(bw, filtered).reshape(slabs * chunks, ROWS, 2 * KB)
        return carry

    lax.fori_loop(0, width, column, 0, unroll=4)

    back = []
    for chunk in range(chunks):
        waits = []
        for step in list(range(1, slabs)) + [0]:
            to = lax.rem(me + step, slabs)
            first = pl.multiple_of(chunk * KB * ROWS + me * (width * ROWS), 8)
            source = send2.at[to * chunks + chunk]
            target = recv2.at[pl.ds(first, width * ROWS)]
            if step == 0:
                copy = pltpu.make_async_copy(source, target, own.at[1, chunk])
            else:
                copy = pltpu.make_async_remote_copy(
                    source, target, s2.at[chunk, step], r2.at[chunk, step],
                    device_id=peer(step), device_id_type=pl.DeviceIdType.MESH,
                )
            copy.start()
            waits.append(copy)
        back.append(waits)
        if chunk == 0:
            shared = []
            for step in range(1, slabs):
                copy = pltpu.make_async_remote_copy(
                    powers.at[me], powers.at[me], sp.at[step], rp.at[step],
                    device_id=peer(step), device_id_type=pl.DeviceIdType.MESH,
                )
                copy.start()
                shared.append(copy)
    for copy in shared:
        copy.wait()

    power = powers[...].reshape(KB, 2 * KB) * (1.0 / KB)
    slots = ids[...]
    wave_y = (slots >> 6) - KCUT
    wave_z = (slots & (KB - 1)) - KCUT
    wave_y = jnp.where(wave_z < 0, -wave_y, wave_y)
    wave_z = jnp.where(wave_z < 0, -wave_z, wave_z)
    count = slots.shape[1]
    row = lax.broadcasted_iota(jnp.int32, (KB, count), 0) - KCUT
    pick_y = jnp.where(row == wave_y, 1.0, 0.0).astype(BF16)
    row = lax.broadcasted_iota(jnp.int32, (2 * KB, count), 0) & (KH - 1)
    high, low = split(power.T)
    rows_of = mm(high, pick_y) + mm(low, pick_y)
    energy[...] = jnp.sum(jnp.where(row == wave_z, rows_of, 0.0), axis=0, keepdims=True)

    for chunk in range(chunks):
        for copy in back[chunk]:
            copy.wait()

        def ungroup(part, carry, chunk=chunk):
            base = chunk * ROWS + part * 4
            pieces = []
            for q in range(4):
                waves = recv2[pl.ds(chunk * KB * ROWS + part * 4 + q, KB, stride=ROWS), :]
                pieces.append(to_points(bw, waves))
            high, low = split(jnp.concatenate(pieces, axis=0))
            both = mm(high, zoh[...]) + mm(low, zoh[...]) + mm(high, zol[...])
            first = src[0, pl.ds(base, 4)].reshape(4 * points, points)
            second = src[1, pl.ds(base, 4)].reshape(4 * points, points)
            total = first * both[:, :points] + second * both[:, points:]
            exch[pl.ds(base, 4)] = total.reshape(4, points, points)
            return carry

        lax.fori_loop(0, ROWS // 4, ungroup, 0)


def from_root(shard, axis, root):
    mine = lax.axis_index(axis) == root
    return lax.psum(jnp.where(mine, shard, jnp.zeros_like(shard)), axis)


def body(orbitals, column_ids, source_ids):
    slabs = lax.axis_size("slab")
    planes, points = orbitals.shape[1], orbitals.shape[2]
    chunks = planes // ROWS
    width = KB // slabs
    sources = jnp.stack([from_root(orbitals[0], "band", source_ids[i]) for i in range(2)])
    vmem = pl.BlockSpec(memory_space=pltpu.VMEM)
    dma = pltpu.SemaphoreType.DMA
    exchange, energy = pl.pallas_call(
        functools.partial(kernel, slabs),
        out_shape=(
            jax.ShapeDtypeStruct((planes, points, points), F32),
            jax.ShapeDtypeStruct((1, column_ids.shape[1]), F32),
        ),
        in_specs=[vmem] * 9,
        out_specs=(vmem, vmem),
        scratch_shapes=[
            pltpu.VMEM((chunks * KB * ROWS, 2 * KB), F32),
            pltpu.VMEM((slabs * chunks, width * ROWS, 2 * KB), F32),
            pltpu.VMEM((slabs * chunks, width * ROWS, 2 * KB), F32),
            pltpu.VMEM((chunks * KB * ROWS, 2 * KB), F32),
            pltpu.VMEM((slabs, width, 2 * KB), F32),
            dma((chunks, slabs)),
            dma((chunks, slabs)),
            dma((chunks, slabs)),
            dma((chunks, slabs)),
            dma((slabs,)),
            dma((slabs,)),
            dma((2, chunks)),
        ],
        compiler_params=pltpu.CompilerParams(
            collective_id=0, has_side_effects=True, vmem_limit_bytes=48 * 1024 * 1024
        ),
        name="exchange_action",
    )(orbitals[0], sources, column_ids, *[jnp.asarray(t) for t in tables(points)])
    return exchange[None], energy


def solution(mesh):
    placed = (P("band", "slab", None, None), P("slab", None), P())
    return jax.shard_map(
        body,
        mesh=mesh,
        in_specs=placed,
        out_specs=(P("band", "slab", None, None), P("band", "slab")),
        check_vma=False,
    )
```

time: 540 us -> 170 us (0.31)
  other arithmetic: 190 us -> 9 us
  local copies, waits for them, and re-layouts: 163 us -> 3.27 us
  Pallas kernels: 0 us -> 58.1 us
  matrix products: 50.4 us -> 0 us
  waiting for transfers between devices: 45.2 us -> 84.1 us
  starting transfers between devices: 38.7 us -> 0.04 us
  blocking collectives: 31.3 us -> 0 us
    scatter-add x4 -> x0, other arithmetic: 86.9 us -> none  [the longest x2 43.8 us: pair_potentials(): empty.at[:, :, send_ids].add(real_back).reshape(pair_count, planes, KB, KB)]
    gather x7 -> x0, local copies, waits for them, and re-layouts: 82.7 us -> none  [the longest x1 34.8 us: body(): packed = listed[ranking]]
    unnamed x4 -> x0, other arithmetic: 67.5 us -> none
    pallas_call x0 -> x1, Pallas kernels: none -> 58.1 us  [body(): pl.pallas_call(functools.partial(kernel, slabs), out_shape=(jax.ShapeDtyp...]
    psum x1, waiting for transfers between devices: 26.7 us -> 84.1 us  [from_root(): return lax.psum(jnp.where(mine, shard, jnp.zeros_like(shard)), axis)]
    dot_general x20 -> x0, matrix products: 50.4 us -> none  [the longest x2 8.86 us: pair_potentials(): jnp.einsum('ay,pxab->pxyb', sin_table, stacked, precision=precise)]
    all_to_all x8 -> x0, starting transfers between devices: 38.7 us -> none  [the longest x2 10.6 us: pair_potentials(): lax.all_to_all(real_cols, 'slab', split_axis=2, concat_axis=1, tiled=True)]
    all_gather x2 -> x0, blocking collectives: 31.3 us -> none  [the longest x1 16.5 us: body(): full_power = lax.all_gather(col_power, 'slab', axis=1, tiled=True)]
  transfers between devices with their start and end apart: 9 -> 1, of which waited for: 3 -> 1; matrix products, arithmetic and copies ran while one was open for 48% -> 0% of each run, Pallas kernels for 0% -> 0%
where the time goes in v1:
time: 170 us
  waiting for transfers between devices  84.1 us (49%)
  Pallas kernels  58.1 us (34%)
  between operations  15.4 us (9%)
  other arithmetic  9 us (5%)
  local copies, waits for them, and re-layouts  3.27 us (2%)
    psum x1, waiting for transfers between devices, from_root(): return lax.psum(jnp.where(mine, shard, jnp.zeros_like(shard)), axis)  84.1 us
    pallas_call x1, Pallas kernels, body(): pl.pallas_call(functools.partial(kernel, slabs), out_shape=(jax.ShapeDtyp...  58.1 us
    another operation x2, other arithmetic, body(): jnp.stack([from_root(orbitals[0], 'band', source_ids[i]) for i in range(2)])  9 us
  transfers between devices with their start and end apart: 1, of which 1 were waited for; matrix products, arithmetic and copies ran while one was open for 0% of the time, Pallas kernels for 0%

profile of v1, /device:TPU:0, one launch (start us, length us, event | category | flops | bytes accessed | tf_op | source)
XLA Modules:
  0.0 169.9 jit_solution(3593171905971765396)
XLA Ops:
  7.2 0.0 all-reduce.3.cloned.1.call-start
  7.2 1.3 fusion
  9.8 4.2 %select_bitcast_fusion.1 = (f32[1,32,128,128]{3,2,1,0:T(8,128)}, f32[1,32,128,128]{3,2,1,0:T(8,128)}) fusion(pred[]{:T(512)S(6)} %eq.6, f32[1,32,128,128]{3,2,1,0:T(8,128)} %param.9, pred[]{:T(512)S(6)} %eq.7), kind=kLoop, calls=%fused_computation.2 | loop fusion | flops 1048576 | bytes 6291458 | tf_op jit(solution)/shard_map/stack | solution.py:234
  14.0 0.0 all-reduce.3.cloned.1.call-update
  14.0 84.1 %all-reduce.3.cloned.1.call-done = (f32[1,32,128,128]{3,2,1,0:T(8,128)}, f32[1,32,128,128]{3,2,1,0:T(8,128)}) async-done(((f32[1,32,128,128]{3,2,1,0:T(8,128)}, f32[1,32,128,128]{3,2,1,0:T(8,128)}), (f32[1,32,128,128]{3,2,1,0:T(8,128)}, f32[1,32,128,128]{3,2,1,0:T(8,128)})) %all-reduce.3.cloned.1.call-update) | async-done | bytes 4194320 | tf_op jit(solution)/shard_map/psum | solution.py:226
  98.1 0.0 copy-start
  98.1 0.0 copy-start.1
  98.1 0.0 copy-start.2
  98.1 0.0 copy-start.3
  98.1 0.0 copy-start.4
  98.1 0.0 copy-start.5
  98.1 0.0 copy-start.6
  98.1 0.0 copy-start.7
  98.2 4.8 %pad_maximum_fusion.src = f32[2,32,128,128]{3,2,1,0:T(8,128)} fusion(f32[1,32,128,128]{3,2,1,0:T(8,128)} %get-tuple-element.6, f32[1,32,128,128]{3,2,1,0:T(8,128)} %get-tuple-element.7), kind=kLoop, calls=%fused_computation | loop fusion | flops 1048576 | bytes 8388608 | tf_op jit(solution)/shard_map/stack | solution.py:234
  103.0 0.0 copy-done
  103.0 0.0 copy-done.1
  103.0 0.0 copy-done.2
  103.0 0.0 copy-done.3
  103.0 0.0 copy-done.4
  103.0 0.0 copy-done.5
  103.0 0.0 copy-done.6
  103.0 0.0 copy-done.7
  103.0 58.1 %exchange_action.1 = (f32[32,128,128]{2,1,0:T(8,128)S(1)}, f32[1,1536]{1,0:T(1,128)S(1)}) custom-call(f32[32,128,128]{2,1,0:T(8,128)S(1)} %bitcast.10, f32[2,32,128,128]{3,2,1,0:T(8,128)} %pad_maximum_fusion.src, s32[1,1536]{1,0:T(1,128)S(1)} %copy-done.7, bf16[256,128]{1,0:T(8,128)(2,1)S(1)} %copy-done.6, bf16[256,128]{1,0:T(8,128)(2,1)S(1)} %copy-done.5, ...), custom_call_target="tpu_custom_call" | custom-call | tf_op jit(solution)/shard_map/exchange_action/pallas_call | solution.py:237
  161.2 1.3 copy.15
  162.5 0.6 copy.16
Async XLA Ops:
  7.2 90.9 %all-reduce.3.cloned.1.call-start = ((), (), s32[]{:S(2)}) async-start(), calls=%async_computation | async-start | bytes 8388608 | tf_op jit(solution)/shard_map/psum | solution.py:226
  98.1 4.9 %copy-start = (f32[1,32,128,128]{3,2,1,0:T(8,128)S(1)}, f32[1,32,128,128]{3,2,1,0:T(8,128)}, u32[]{:S(2)}) copy-start(f32[1,32,128,128]{3,2,1,0:T(8,128)} %param.9) | copy-start | bytes 6291460
  98.1 4.9 %copy-start.1 = (bf16[128,256]{1,0:T(8,128)(2,1)S(1)}, bf16[128,256]{1,0:T(8,128)(2,1)}, u32[]{:S(2)}) copy-start(bf16[128,256]{1,0:T(8,128)(2,1)} %constant.25.clone.zol) | copy-start | bytes 196612
  98.1 4.9 %copy-start.2 = (bf16[128,256]{1,0:T(8,128)(2,1)S(1)}, bf16[128,256]{1,0:T(8,128)(2,1)}, u32[]{:S(2)}) copy-start(bf16[128,256]{1,0:T(8,128)(2,1)} %constant.24.clone.zoh) | copy-start | bytes 196612
  98.1 4.9 %copy-start.3 = (bf16[256,128]{1,0:T(8,128)(2,1)S(1)}, bf16[256,128]{1,0:T(8,128)(2,1)}, u32[]{:S(2)}) copy-start(bf16[256,128]{1,0:T(8,128)(2,1)} %constant.23.clone.zil) | copy-start | bytes 196612
  98.1 4.9 %copy-start.4 = (bf16[256,128]{1,0:T(8,128)(2,1)S(1)}, bf16[256,128]{1,0:T(8,128)(2,1)}, u32[]{:S(2)}) copy-start(bf16[256,128]{1,0:T(8,128)(2,1)} %constant.22.clone.zih) | copy-start | bytes 196612
  98.1 4.9 %copy-start.5 = (bf16[256,128]{1,0:T(8,128)(2,1)S(1)}, bf16[256,128]{1,0:T(8,128)(2,1)}, u32[]{:S(2)}) copy-start(bf16[256,128]{1,0:T(8,128)(2,1)} %constant.21.clone.bw) | copy-start | bytes 196612
  98.1 4.9 %copy-start.6 = (bf16[256,128]{1,0:T(8,128)(2,1)S(1)}, bf16[256,128]{1,0:T(8,128)(2,1)}, u32[]{:S(2)}) copy-start(bf16[256,128]{1,0:T(8,128)(2,1)} %constant.20.clone.fw) | copy-start | bytes 196612
  98.1 4.9 %copy-start.7 = (s32[1,1536]{1,0:T(1,128)S(1)}, s32[1,1536]{1,0:T(1,128)}, u32[]{:S(2)}) copy-start(s32[1,1536]{1,0:T(1,128)} %ids.1) | copy-start | bytes 18436
Sparse Core Ops, SparseCore 0:
  14.2 83.9 all-reduce.2

commit v2 on v1

--- a/solution.py
+++ b/solution.py
@@ -13,6 +13,7 @@
 KB = 64
 KH = 32
 ROWS = 8
+STAGES = 6
 F32 = jnp.float32
 BF16 = jnp.bfloat16
 
@@ -88,10 +89,99 @@
     return left_apply(table_ref, jnp.concatenate([value, swap_parts(value, -1.0)], axis=0))
 
 
-def kernel(
-    slabs, orb, src, ids, fw, bw, zih, zil, zoh, zol, exch, energy,
-    send1, recv1, send2, recv2, powers, s1, r1, s2, r2, sp, rp, own,
-):
+def spread(orb, owners, src, half, work, near, far, ssem, rsem):
+    points = orb.shape[1]
+    part = points // 2
+    band = lax.axis_index("band")
+    bits = [lax.rem(band, 2), lax.rem(band // 2, 2), band // 4]
+    other = [band + weight * (1 - 2 * bit) for weight, bit in zip((1, 2, 4), bits)]
+    mine = bits[0] * part
+    axes = ((1, 2), (2, 1))
+
+    def rows(start, size):
+        return pl.ds(pl.multiple_of(start, 8), size)
+
+    def local(which):
+        one, two = axes[which]
+        keep = which * (part // 2) + bits[one] * (part // 4)
+        drop = which * (part // 2) + (1 - bits[one]) * (part // 4)
+        last = keep + bits[two] * (part // 8)
+        give = keep + (1 - bits[two]) * (part // 8)
+        return keep, drop, last, give
+
+    def copy(source, target, chunk, number, axis):
+        return pltpu.make_async_remote_copy(
+            source, target, ssem.at[chunk, number], rsem.at[chunk, number],
+            device_id={"band": other[axis]}, device_id_type=pl.DeviceIdType.MESH,
+        )
+
+    def choose(source, axis, kept, arrived):
+        owner = jnp.zeros(kept.shape, jnp.int32) + owners[source]
+        return jnp.where(((owner >> axis) & 1) == bits[axis], kept, arrived)
+
+    def start(chunk, stage):
+        span = pl.ds(chunk * ROWS, ROWS)
+        if stage == 0:
+            source = orb.at[span, rows((1 - bits[0]) * part, part)]
+            copies = [copy(source, half.at[span], chunk, 0, 0)]
+        else:
+            copies = []
+            for which in range(2):
+                one, two = axes[which]
+                keep, drop, last, give = local(which)
+                number = 1 + which * 5 + stage - 1
+                if stage == 1:
+                    source = work.at[:, span, rows(drop, part // 4)]
+                    made = copy(source, near.at[which, :, span], chunk, number, one)
+                elif stage == 2:
+                    source = work.at[:, span, rows(give, part // 8)]
+                    made = copy(source, far.at[which, :, span], chunk, number, two)
+                else:
+                    if stage == 3:
+                        begin, size, axis = last, part // 8, two
+                    elif stage == 4:
+                        begin, size, axis = keep, part // 4, one
+                    else:
+                        begin, size, axis = which * (part // 2), part // 2, 0
+                    place = src.at[:, span, rows(mine + begin, size)]
+                    made = copy(place, place, chunk, number, axis)
+                copies.append(made)
+        for made in copies:
+            made.start()
+        return copies
+
+    def resolve(chunk, stage):
+        span = pl.ds(chunk * ROWS, ROWS)
+        for source in range(2):
+            if stage == 0:
+                kept = orb[span, rows(mine, part), :]
+                work[source, span] = choose(source, 0, kept, half[span])
+                continue
+            for which in range(2):
+                one, two = axes[which]
+                keep, drop, last, give = local(which)
+                if stage == 1:
+                    place = rows(keep, part // 4)
+                    kept = work[source, span, place, :]
+                    work[source, span, place, :] = choose(source, one, kept, near[which, source, span])
+                elif stage == 2:
+                    kept = work[source, span, rows(last, part // 8), :]
+                    arrived = far[which, source, span]
+                    src[source, span, rows(mine + last, part // 8), :] = choose(source, two, kept, arrived)
+
+    return other, start, resolve
+
+
+def kernel(slabs, spreading, *refs):
+    if spreading:
+        orb, owners, ids, fw, bw, zih, zil, zoh, zol, exch, energy = refs[:11]
+        send1, recv1, send2, recv2, powers, s1, r1, s2, r2, sp, rp, own = refs[11:23]
+        src, half, work, near, far, ssem, rsem = refs[23:]
+        others, start, resolve = spread(orb, owners, src, half, work, near, far, ssem, rsem)
+    else:
+        orb, src, ids, fw, bw, zih, zil, zoh, zol, exch, energy = refs[:11]
+        send1, recv1, send2, recv2, powers, s1, r1, s2, r2, sp, rp, own = refs[11:]
+        others = []
     planes, points = orb.shape[0], orb.shape[1]
     chunks = planes // ROWS
     width = KB // slabs
@@ -103,10 +193,15 @@
     barrier = pltpu.get_barrier_semaphore()
     for step in range(1, slabs):
         pl.semaphore_signal(barrier, inc=1, device_id=peer(step), device_id_type=pl.DeviceIdType.MESH)
-    pl.semaphore_wait(barrier, slabs - 1)
+    for device in others:
+        pl.semaphore_signal(
+            barrier, inc=1, device_id={"band": device}, device_id_type=pl.DeviceIdType.MESH
+        )
+    pl.semaphore_wait(barrier, slabs - 1 + len(others))
 
     forward = []
-    for chunk in range(chunks):
+
+    def advance(chunk):
 
         def group(part, carry, chunk=chunk):
             base = chunk * ROWS + part * 4
@@ -136,6 +231,30 @@
                 )
             copy.start()
             forward.append(copy)
+
+    if spreading:
+        sent = []
+        flying = {}
+        for tick in range(chunks + STAGES):
+            for stage in reversed(range(STAGES)):
+                chunk = tick - stage
+                if not 0 <= chunk < chunks:
+                    continue
+                if stage > 0:
+                    for copy in flying[chunk]:
+                        copy.wait_recv()
+                    resolve(chunk, stage - 1)
+                flying[chunk] = start(chunk, stage)
+                sent.extend(flying[chunk])
+            chunk = tick - STAGES
+            if 0 <= chunk < chunks:
+                for copy in flying[chunk]:
+                    copy.wait_recv()
+                advance(chunk)
+    else:
+        sent = []
+        for chunk in range(chunks):
+            advance(chunk)
     for copy in forward:
         copy.wait()
 
@@ -219,6 +338,8 @@
             return carry
 
         lax.fori_loop(0, ROWS // 4, ungroup, 0)
+    for copy in sent:
+        copy.wait_send()
 
 
 def from_root(shard, axis, root):
@@ -231,16 +352,33 @@
     planes, points = orbitals.shape[1], orbitals.shape[2]
     chunks = planes // ROWS
     width = KB // slabs
-    sources = jnp.stack([from_root(orbitals[0], "band", source_ids[i]) for i in range(2)])
+    bands = lax.axis_size("band")
+    spreading = bands == 8 and points % 128 == 0
     vmem = pl.BlockSpec(memory_space=pltpu.VMEM)
     dma = pltpu.SemaphoreType.DMA
+    if spreading:
+        sources = source_ids
+        extra = [
+            pltpu.VMEM((2, planes, points, points), F32),
+            pltpu.VMEM((planes, points // 2, points), F32),
+            pltpu.VMEM((2, planes, points // 2, points), F32),
+            pltpu.VMEM((2, 2, planes, points // 8, points), F32),
+            pltpu.VMEM((2, 2, planes, points // 16, points), F32),
+            dma((chunks, 11)),
+            dma((chunks, 11)),
+        ]
+        place = pl.BlockSpec(memory_space=pltpu.SMEM)
+    else:
+        sources = jnp.stack([from_root(orbitals[0], "band", source_ids[i]) for i in range(2)])
+        extra = []
+        place = vmem
     exchange, energy = pl.pallas_call(
-        functools.partial(kernel, slabs),
+        functools.partial(kernel, slabs, spreading),
         out_shape=(
             jax.ShapeDtypeStruct((planes, points, points), F32),
             jax.ShapeDtypeStruct((1, column_ids.shape[1]), F32),
         ),
-        in_specs=[vmem] * 9,
+        in_specs=[vmem, place] + [vmem] * 7,
         out_specs=(vmem, vmem),
         scratch_shapes=[
             pltpu.VMEM((chunks * KB * ROWS, 2 * KB), F32),
@@ -255,6 +393,7 @@
             dma((slabs,)),
             dma((slabs,)),
             dma((2, chunks)),
+            *extra,
         ],
         compiler_params=pltpu.CompilerParams(
             collective_id=0, has_side_effects=True, vmem_limit_bytes=48 * 1024 * 1024

time: 170 us -> 102 us (0.60)
  waiting for transfers between devices: 84.1 us -> 0 us
  Pallas kernels: 58.1 us -> 90.5 us
  between operations: 15.4 us -> 0.66 us
  other arithmetic: 9 us -> 0 us
  local copies, waits for them, and re-layouts: 3.27 us -> 9.88 us
    psum x1 -> x0, waiting for transfers between devices: 84.1 us -> none  [from_root(): return lax.psum(jnp.where(mine, shard, jnp.zeros_like(shard)), axis)]
    pallas_call x1, Pallas kernels: 58.1 us -> 90.5 us  [body(): pl.pallas_call(functools.partial(kernel, slabs, spreading), out_shape=(ja...]
    another operation x2 -> x0, other arithmetic: 9 us -> none  [body(): jnp.stack([from_root(orbitals[0], 'band', source_ids[i]) for i in range(2)])]
    unnamed x18 -> x20, local copies, waits for them, and re-layouts: 1.95 us -> 9.88 us
  transfers between devices with their start and end apart: 1 -> 0, of which waited for: 1 -> 0; matrix products, arithmetic and copies ran while one was open for 0% -> 0% of each run, Pallas kernels for 0% -> 0%
where the time goes in v2:
time: 102 us; the launch traced here: 101 us
  Pallas kernels  90.5 us (89%)
  local copies, waits for them, and re-layouts  9.88 us (10%)
    pallas_call x1, Pallas kernels, body(): pl.pallas_call(functools.partial(kernel, slabs, spreading), out_shape=(ja...  90.5 us
    unnamed x20, local copies, waits for them, and re-layouts  9.88 us

profile of v2, /device:TPU:0, one launch (start us, length us, event | category | flops | bytes accessed | tf_op | source)
XLA Modules:
  0.0 101.1 jit_solution(13060974036848146021)
XLA Ops:
  0.6 0.0 copy-start
  0.6 1.6 %copy-done = f32[1,32,128,128]{3,2,1,0:T(8,128)S(1)} copy-done((f32[1,32,128,128]{3,2,1,0:T(8,128)S(1)}, f32[1,32,128,128]{3,2,1,0:T(8,128)}, u32[]{:S(2)}) %copy-start) | copy-done | bytes 2097176
  2.2 0.0 copy-start.1
  2.2 0.8 copy-done.1
  3.1 0.0 copy-start.2
  3.1 0.8 copy-done.2
  3.9 0.0 copy-start.3
  3.9 0.8 copy-done.3
  4.7 0.0 copy-start.4
  4.7 0.8 copy-done.4
  5.6 0.0 copy-start.5
  5.6 0.8 copy-done.5
  6.4 0.0 copy-start.6
  6.4 0.8 copy-done.6
  7.3 0.0 copy-start.7
  7.3 0.7 copy-done.7
  8.0 0.0 copy-start.8
  8.0 0.7 copy-done.8
  8.6 90.5 %exchange_action.1 = (f32[32,128,128]{2,1,0:T(8,128)S(1)}, f32[1,1536]{1,0:T(1,128)S(1)}) custom-call(f32[32,128,128]{2,1,0:T(8,128)S(1)} %bitcast.2, s32[2]{0:T(128)S(1)} %copy-done.8, s32[1,1536]{1,0:T(1,128)S(1)} %copy-done.7, bf16[256,128]{1,0:T(8,128)(2,1)S(1)} %copy-done.6, bf16[256,128]{1,0:T(8,128)(2,1)S(1)} %copy-done.5, ...), custom_call_target="tpu_custom_call" | custom-call | tf_op jit(solution)/shard_map/exchange_action/pallas_call | solution.py:375
  99.2 1.3 %copy.13 = f32[1,32,128,128]{3,2,1,0:T(8,128)} copy(f32[1,32,128,128]{3,2,1,0:T(8,128)S(1)} %bitcast.3) | data formatting | bytes 4194304
  100.5 0.6 copy.14
Async XLA Ops:
  0.6 1.6 %copy-start = (f32[1,32,128,128]{3,2,1,0:T(8,128)S(1)}, f32[1,32,128,128]{3,2,1,0:T(8,128)}, u32[]{:S(2)}) copy-start(f32[1,32,128,128]{3,2,1,0:T(8,128)} %param.9) | copy-start | bytes 6291460
  2.2 0.8 copy-start.1
  3.1 0.8 copy-start.2
  3.9 0.8 copy-start.3
  4.7 0.8 copy-start.4
  5.6 0.8 copy-start.5
  6.4 0.8 copy-start.6
  7.3 0.7 copy-start.7
  8.0 0.7 copy-start.8

commit v3 on v2

--- a/solution.py
+++ b/solution.py
@@ -14,6 +14,7 @@
 KH = 32
 ROWS = 8
 STAGES = 6
+PIECE = 4
 F32 = jnp.float32
 BF16 = jnp.bfloat16
 
@@ -54,6 +55,7 @@
     bh, bl = halves(backward)
     ih, il = halves(into)
     oh, ol = halves(out)
+    oh, ol = [np.concatenate(np.split(table, 2, axis=1), axis=0) for table in (oh, ol)]
     return (np.concatenate([fh, fl], 0), np.concatenate([bh, bl], 0), ih, il, oh, ol)
 
 
@@ -89,7 +91,7 @@
     return left_apply(table_ref, jnp.concatenate([value, swap_parts(value, -1.0)], axis=0))
 
 
-def spread(orb, owners, src, half, work, near, far, ssem, rsem):
+def spread(far_orb, orb, owners, src, half, work, near, far, ssem, rsem):
     points = orb.shape[1]
     part = points // 2
     band = lax.axis_index("band")
@@ -120,9 +122,9 @@
         return jnp.where(((owner >> axis) & 1) == bits[axis], kept, arrived)
 
     def start(chunk, stage):
-        span = pl.ds(chunk * ROWS, ROWS)
+        span = pl.ds(chunk * PIECE, PIECE)
         if stage == 0:
-            source = orb.at[span, rows((1 - bits[0]) * part, part)]
+            source = far_orb.at[span, rows((1 - bits[0]) * part, part)]
             copies = [copy(source, half.at[span], chunk, 0, 0)]
         else:
             copies = []
@@ -151,7 +153,7 @@
         return copies
 
     def resolve(chunk, stage):
-        span = pl.ds(chunk * ROWS, ROWS)
+        span = pl.ds(chunk * PIECE, PIECE)
         for source in range(2):
             if stage == 0:
                 kept = orb[span, rows(mine, part), :]
@@ -174,13 +176,24 @@
 
 def kernel(slabs, spreading, *refs):
     if spreading:
-        orb, owners, ids, fw, bw, zih, zil, zoh, zol, exch, energy = refs[:11]
-        send1, recv1, send2, recv2, powers, s1, r1, s2, r2, sp, rp, own = refs[11:23]
-        src, half, work, near, far, ssem, rsem = refs[23:]
-        others, start, resolve = spread(orb, owners, src, half, work, near, far, ssem, rsem)
+        owners, exch, energy = refs[1], refs[9], refs[10]
+        send1, recv1, send2, recv2, powers, s1, r1, s2, r2, sp, rp, own, made, stored = refs[11:25]
+        src, half, work, near, far, ssem, rsem = refs[25:32]
+        placed, loaded = refs[32:40], refs[40]
+        orb, ids, fw, bw, zih, zil, zoh, zol = placed
+        outside = (refs[0],) + refs[2:9]
+        loads = [
+            pltpu.make_async_copy(there, here, loaded.at[number])
+            for number, (there, here) in enumerate(zip(outside, placed))
+        ]
+        for load in loads:
+            load.start()
+        others, start, resolve = spread(
+            refs[0], orb, owners, src, half, work, near, far, ssem, rsem
+        )
     else:
         orb, src, ids, fw, bw, zih, zil, zoh, zol, exch, energy = refs[:11]
-        send1, recv1, send2, recv2, powers, s1, r1, s2, r2, sp, rp, own = refs[11:]
+        send1, recv1, send2, recv2, powers, s1, r1, s2, r2, sp, rp, own, made, stored = refs[11:]
         others = []
     planes, points = orb.shape[0], orb.shape[1]
     chunks = planes // ROWS
@@ -235,10 +248,15 @@
     if spreading:
         sent = []
         flying = {}
-        for tick in range(chunks + STAGES):
+        pieces = planes // PIECE
+        each = ROWS // PIECE
+        for tick in range(pieces + STAGES):
+            if tick == 1:
+                for load in loads:
+                    load.wait()
             for stage in reversed(range(STAGES)):
                 chunk = tick - stage
-                if not 0 <= chunk < chunks:
+                if not 0 <= chunk < pieces:
                     continue
                 if stage > 0:
                     for copy in flying[chunk]:
@@ -247,10 +265,11 @@
                 flying[chunk] = start(chunk, stage)
                 sent.extend(flying[chunk])
             chunk = tick - STAGES
-            if 0 <= chunk < chunks:
+            if 0 <= chunk < pieces:
                 for copy in flying[chunk]:
                     copy.wait_recv()
-                advance(chunk)
+                if chunk % each == each - 1:
+                    advance(chunk // each)
     else:
         sent = []
         for chunk in range(chunks):
@@ -319,6 +338,7 @@
     rows_of = mm(high, pick_y) + mm(low, pick_y)
     energy[...] = jnp.sum(jnp.where(row == wave_z, rows_of, 0.0), axis=0, keepdims=True)
 
+    stores = []
     for chunk in range(chunks):
         for copy in back[chunk]:
             copy.wait()
@@ -330,14 +350,21 @@
                 waves = recv2[pl.ds(chunk * KB * ROWS + part * 4 + q, KB, stride=ROWS), :]
                 pieces.append(to_points(bw, waves))
             high, low = split(jnp.concatenate(pieces, axis=0))
-            both = mm(high, zoh[...]) + mm(low, zoh[...]) + mm(high, zol[...])
+            top = jnp.concatenate([zoh[:points, :], zoh[points:, :]], axis=1)
+            rest = jnp.concatenate([zol[:points, :], zol[points:, :]], axis=1)
+            both = mm(high, top) + mm(low, top) + mm(high, rest)
             first = src[0, pl.ds(base, 4)].reshape(4 * points, points)
             second = src[1, pl.ds(base, 4)].reshape(4 * points, points)
             total = first * both[:, :points] + second * both[:, points:]
-            exch[pl.ds(base, 4)] = total.reshape(4, points, points)
+            made[pl.ds(base, 4)] = total.reshape(4, points, points)
             return carry
 
         lax.fori_loop(0, ROWS // 4, ungroup, 0)
+        span = pl.ds(chunk * ROWS, ROWS)
+        stores.append(pltpu.make_async_copy(made.at[span], exch.at[span], stored.at[chunk]))
+        stores[-1].start()
+    for copy in stores:
+        copy.wait()
     for copy in sent:
         copy.wait_send()
 
@@ -356,6 +383,7 @@
     spreading = bands == 8 and points % 128 == 0
     vmem = pl.BlockSpec(memory_space=pltpu.VMEM)
     dma = pltpu.SemaphoreType.DMA
+    fixed = [jnp.asarray(table) for table in tables(points)]
     if spreading:
         sources = source_ids
         extra = [
@@ -364,22 +392,27 @@
             pltpu.VMEM((2, planes, points // 2, points), F32),
             pltpu.VMEM((2, 2, planes, points // 8, points), F32),
             pltpu.VMEM((2, 2, planes, points // 16, points), F32),
-            dma((chunks, 11)),
-            dma((chunks, 11)),
+            dma((planes // PIECE, 11)),
+            dma((planes // PIECE, 11)),
+            pltpu.VMEM((planes, points, points), F32),
+            pltpu.VMEM(column_ids.shape, jnp.int32),
+            *[pltpu.VMEM(table.shape, BF16) for table in fixed],
+            dma((8,)),
         ]
+        home = pl.BlockSpec(memory_space=pltpu.HBM)
         place = pl.BlockSpec(memory_space=pltpu.SMEM)
     else:
         sources = jnp.stack([from_root(orbitals[0], "band", source_ids[i]) for i in range(2)])
         extra = []
-        place = vmem
+        home = place = vmem
     exchange, energy = pl.pallas_call(
         functools.partial(kernel, slabs, spreading),
         out_shape=(
             jax.ShapeDtypeStruct((planes, points, points), F32),
             jax.ShapeDtypeStruct((1, column_ids.shape[1]), F32),
         ),
-        in_specs=[vmem, place] + [vmem] * 7,
-        out_specs=(vmem, vmem),
+        in_specs=[home, place] + [home] * 7,
+        out_specs=(pl.BlockSpec(memory_space=pltpu.HBM), vmem),
         scratch_shapes=[
             pltpu.VMEM((chunks * KB * ROWS, 2 * KB), F32),
             pltpu.VMEM((slabs * chunks, width * ROWS, 2 * KB), F32),
@@ -393,13 +426,15 @@
             dma((slabs,)),
             dma((slabs,)),
             dma((2, chunks)),
+            pltpu.VMEM((planes, points, points), F32),
+            dma((chunks,)),
             *extra,
         ],
         compiler_params=pltpu.CompilerParams(
-            collective_id=0, has_side_effects=True, vmem_limit_bytes=48 * 1024 * 1024
+            collective_id=0, has_side_effects=True, vmem_limit_bytes=63 * 1024 * 1024
         ),
         name="exchange_action",
-    )(orbitals[0], sources, column_ids, *[jnp.asarray(t) for t in tables(points)])
+    )(orbitals[0], sources, column_ids, *fixed)
     return exchange[None], energy
 
 

time: 102 us -> 95.6 us (0.937)
  local copies, waits for them, and re-layouts: 9.88 us -> 3.74 us
    unnamed x20 -> x4, local copies, waits for them, and re-layouts: 9.88 us -> 3.74 us
where the time goes in v3:
time: 95.6 us; the launch traced here: 95.4 us
  Pallas kernels  91 us (95%)
  local copies, waits for them, and re-layouts  3.74 us (4%)
    pallas_call x1, Pallas kernels, body(): pl.pallas_call(functools.partial(kernel, slabs, spreading), out_shape=(ja...  91 us
    unnamed x4, local copies, waits for them, and re-layouts  3.74 us

profile of v3, /device:TPU:0, one launch (start us, length us, event | category | flops | bytes accessed | tf_op | source)
XLA Modules:
  0.0 95.4 jit_solution(15195694907972745069)
XLA Ops:
  0.6 91.0 %exchange_action.1 = (f32[32,128,128]{2,1,0:T(8,128)}, f32[1,1536]{1,0:T(1,128)}) custom-call(f32[32,128,128]{2,1,0:T(8,128)} %bitcast.2, s32[2]{0:T(128)} %refs_1_.1, s32[1,1536]{1,0:T(1,128)} %refs_2_.1, bf16[256,128]{1,0:T(8,128)(2,1)} %constant.12.clone.refs_3_, bf16[256,128]{1,0:T(8,128)(2,1)} %constant.13.clone.refs_4_, ...), custom_call_target="tpu_custom_call" | custom-call | tf_op jit(solution)/shard_map/exchange_action/pallas_call | solution.py:408
  91.7 0.0 copy-start
  91.7 3.1 %copy.13 = f32[1,32,128,128]{3,2,1,0:T(8,128)} copy(f32[1,32,128,128]{3,2,1,0:T(8,128)} %bitcast.3) | data formatting | bytes 4194304
  94.8 0.0 copy-done
  94.8 0.6 copy.14
Async XLA Ops:
  91.7 3.2 %copy-start = (f32[1,1536]{1,0:T(1,128)S(1)}, f32[1,1536]{1,0:T(1,128)}, u32[]{:S(2)}) copy-start(f32[1,1536]{1,0:T(1,128)} %get-tuple-element.9) | copy-start | bytes 18436

commit v4 on v3

--- a/solution.py
+++ b/solution.py
@@ -292,35 +292,34 @@
         send2[:, rows, :] = to_points(bw, filtered).reshape(slabs * chunks, ROWS, 2 * KB)
         return carry
 
-    lax.fori_loop(0, width, column, 0, unroll=4)
-
-    back = []
-    for chunk in range(chunks):
-        waits = []
-        for step in list(range(1, slabs)) + [0]:
-            to = lax.rem(me + step, slabs)
-            first = pl.multiple_of(chunk * KB * ROWS + me * (width * ROWS), 8)
-            source = send2.at[to * chunks + chunk]
-            target = recv2.at[pl.ds(first, width * ROWS)]
-            if step == 0:
-                copy = pltpu.make_async_copy(source, target, own.at[1, chunk])
-            else:
-                copy = pltpu.make_async_remote_copy(
-                    source, target, s2.at[chunk, step], r2.at[chunk, step],
-                    device_id=peer(step), device_id_type=pl.DeviceIdType.MESH,
-                )
-            copy.start()
-            waits.append(copy)
-        back.append(waits)
-        if chunk == 0:
-            shared = []
-            for step in range(1, slabs):
-                copy = pltpu.make_async_remote_copy(
-                    powers.at[me], powers.at[me], sp.at[step], rp.at[step],
-                    device_id=peer(step), device_id_type=pl.DeviceIdType.MESH,
-                )
+    back = [[] for _ in range(chunks)]
+    few = width // 2
+    for turn in range(2):
+        lax.fori_loop(turn * few, (turn + 1) * few, column, 0, unroll=4)
+        for chunk in range(chunks):
+            for step in list(range(1, slabs)) + [0]:
+                to = lax.rem(me + step, slabs)
+                begin = chunk * KB * ROWS + me * (width * ROWS) + turn * (few * ROWS)
+                source = send2.at[to * chunks + chunk, pl.ds(turn * few * ROWS, few * ROWS)]
+                target = recv2.at[pl.ds(pl.multiple_of(begin, 8), few * ROWS)]
+                if step == 0:
+                    copy = pltpu.make_async_copy(source, target, own.at[1 + turn, chunk])
+                else:
+                    copy = pltpu.make_async_remote_copy(
+                        source, target, s2.at[turn * chunks + chunk, step],
+                        r2.at[turn * chunks + chunk, step],
+                        device_id=peer(step), device_id_type=pl.DeviceIdType.MESH,
+                    )
                 copy.start()
-                shared.append(copy)
+                back[chunk].append(copy)
+    shared = []
+    for step in range(1, slabs):
+        copy = pltpu.make_async_remote_copy(
+            powers.at[me], powers.at[me], sp.at[step], rp.at[step],
+            device_id=peer(step), device_id_type=pl.DeviceIdType.MESH,
+        )
+        copy.start()
+        shared.append(copy)
     for copy in shared:
         copy.wait()
 
@@ -421,11 +420,11 @@
             pltpu.VMEM((slabs, width, 2 * KB), F32),
             dma((chunks, slabs)),
             dma((chunks, slabs)),
-            dma((chunks, slabs)),
-            dma((chunks, slabs)),
+            dma((2 * chunks, slabs)),
+            dma((2 * chunks, slabs)),
             dma((slabs,)),
             dma((slabs,)),
-            dma((2, chunks)),
+            dma((3, chunks)),
             pltpu.VMEM((planes, points, points), F32),
             dma((chunks,)),
             *extra,

time: 95.6 us -> 99.7 us (1.043)
  Pallas kernels: 91 us -> 95.1 us
    pallas_call x1, Pallas kernels: 91 us -> 95.1 us  [body(): pl.pallas_call(functools.partial(kernel, slabs, spreading), out_shape=(ja...]
where the time goes in v4:
time: 99.7 us; the launch traced here: 99.5 us
  Pallas kernels  95.1 us (95%)
  local copies, waits for them, and re-layouts  3.74 us (4%)
    pallas_call x1, Pallas kernels, body(): pl.pallas_call(functools.partial(kernel, slabs, spreading), out_shape=(ja...  95.1 us
    unnamed x4, local copies, waits for them, and re-layouts  3.74 us

profile of v4, /device:TPU:0, one launch (start us, length us, event | category | flops | bytes accessed | tf_op | source)
XLA Modules:
  0.0 99.5 jit_solution(2873273797352993785)
XLA Ops:
  0.6 95.1 %exchange_action.1 = (f32[32,128,128]{2,1,0:T(8,128)}, f32[1,1536]{1,0:T(1,128)}) custom-call(f32[32,128,128]{2,1,0:T(8,128)} %bitcast.2, s32[2]{0:T(128)} %refs_1_.1, s32[1,1536]{1,0:T(1,128)} %refs_2_.1, bf16[256,128]{1,0:T(8,128)(2,1)} %constant.12.clone.refs_3_, bf16[256,128]{1,0:T(8,128)(2,1)} %constant.13.clone.refs_4_, ...), custom_call_target="tpu_custom_call" | custom-call | tf_op jit(solution)/shard_map/exchange_action/pallas_call | solution.py:407
  95.8 0.0 copy-start
  95.8 3.1 %copy.13 = f32[1,32,128,128]{3,2,1,0:T(8,128)} copy(f32[1,32,128,128]{3,2,1,0:T(8,128)} %bitcast.3) | data formatting | bytes 4194304
  98.9 0.0 copy-done
  98.9 0.6 copy.14
Async XLA Ops:
  95.8 3.2 %copy-start = (f32[1,1536]{1,0:T(1,128)S(1)}, f32[1,1536]{1,0:T(1,128)}, u32[]{:S(2)}) copy-start(f32[1,1536]{1,0:T(1,128)} %get-tuple-element.9) | copy-start | bytes 18436

commit v5 on v3

--- a/solution.py
+++ b/solution.py
@@ -14,7 +14,7 @@
 KH = 32
 ROWS = 8
 STAGES = 6
-PIECE = 4
+PIECE = 8
 F32 = jnp.float32
 BF16 = jnp.bfloat16
 

time: 95.6 us -> 96.9 us (1.014)
  Pallas kernels: 91 us -> 92.4 us
    pallas_call x1, Pallas kernels: 91 us -> 92.4 us  [body(): pl.pallas_call(functools.partial(kernel, slabs, spreading), out_shape=(ja...]
where the time goes in v5:
time: 96.9 us; the launch traced here: 96.8 us
  Pallas kernels  92.4 us (95%)
  local copies, waits for them, and re-layouts  3.74 us (4%)
    pallas_call x1, Pallas kernels, body(): pl.pallas_call(functools.partial(kernel, slabs, spreading), out_shape=(ja...  92.4 us
    unnamed x4, local copies, waits for them, and re-layouts  3.74 us

profile of v5, /device:TPU:0, one launch (start us, length us, event | category | flops | bytes accessed | tf_op | source)
XLA Modules:
  0.0 96.8 jit_solution(14014486012597734941)
XLA Ops:
  0.6 92.4 %exchange_action.1 = (f32[32,128,128]{2,1,0:T(8,128)}, f32[1,1536]{1,0:T(1,128)}) custom-call(f32[32,128,128]{2,1,0:T(8,128)} %bitcast.2, s32[2]{0:T(128)} %refs_1_.1, s32[1,1536]{1,0:T(1,128)} %refs_2_.1, bf16[256,128]{1,0:T(8,128)(2,1)} %constant.12.clone.refs_3_, bf16[256,128]{1,0:T(8,128)(2,1)} %constant.13.clone.refs_4_, ...), custom_call_target="tpu_custom_call" | custom-call | tf_op jit(solution)/shard_map/exchange_action/pallas_call | solution.py:408
  93.0 0.0 copy-start
  93.0 3.1 %copy.13 = f32[1,32,128,128]{3,2,1,0:T(8,128)} copy(f32[1,32,128,128]{3,2,1,0:T(8,128)} %bitcast.3) | data formatting | bytes 4194304
  96.2 0.0 copy-done
  96.2 0.6 copy.14
Async XLA Ops:
  93.0 3.2 %copy-start = (f32[1,1536]{1,0:T(1,128)S(1)}, f32[1,1536]{1,0:T(1,128)}, u32[]{:S(2)}) copy-start(f32[1,1536]{1,0:T(1,128)} %get-tuple-element.9) | copy-start | bytes 18436
